TPU v7x, 32 devices: a whole 2x2x4 slice. The times are simulated.
32 devices in a mesh: pix: 16 (over z, y, x), tm: 2 (over core).
Axes of the slice: x: 2, y: 2, z: 4, core: 2. Of those that a mesh axis runs over, the one named last changes fastest.
Arguments:
- movie: bfloat16 [32768, 512], P('pix', 'tm'), may hold values from -6 to 6
- traces: bfloat16 [512, 512], P('pix', 'tm'), may hold values from 0 to 2
- footprints: bfloat16 [4096, 128], P('pix'), may hold values from 0 to 0.2
- slot_block: int32 [4096], P('pix'), may hold values from 0 to 15
- slot_neuron: int32 [4096], P('pix'), may hold values from 0 to 31
- bucket_fill: int32 [16, 16], P('pix'), may hold values from 1 to 16, as said below
Outputs:
- traces_new: bfloat16 [512, 512], P('pix', 'tm')
- footprints_new: float32 [4096, 128], P('pix')
Inputs may be any that keep to these rules, and one draw needn't show every extreme that they name: `bucket_fill`: A tile has at most 16 used slots for one owner; in every draw some owner gets 16 from every tile, and every tile fills 16 for some owner.
All inputs are finite; a program needn't handle non-finite values.
Results may differ from a plain program's by a relative error of at most 0.0049.
Values may be sent and summed in bfloat16 or wider, within the bound.
A program may use at most 64 MiB of HBM per device.

v0:
```python
import jax
import jax.numpy as jnp
from jax import lax
from jax.sharding import PartitionSpec as P

BLOCK = 128


def local(movie, traces, footprints, slot_block, slot_neuron, bucket_fill):
    pix_count = lax.axis_size("pix")
    slot_total = footprints.shape[0]
    capacity = slot_total // pix_count
    neur_local = traces.shape[0]
    block_count = movie.shape[0] // BLOCK
    slot_index = jnp.arange(slot_total, dtype=jnp.int32)
    bucket_of = slot_index // capacity
    position = slot_index % capacity
    owner_match = bucket_of[:, None] == jnp.arange(pix_count, dtype=jnp.int32)[None, :]
    fill_slot = jnp.sum(jnp.where(owner_match, bucket_fill[0][None, :], 0), axis=1)
    usable = position < fill_slot
    masked = footprints * usable[:, None].astype(jnp.bfloat16)
    block_pick = slot_block[:, None] == jnp.arange(block_count, dtype=jnp.int32)[None, :]
    dense_map = (block_pick.astype(jnp.bfloat16)[:, :, None] * masked[:, None, :]).reshape(
        slot_total, block_count * BLOCK
    )
    asked_ids = lax.all_to_all(
        slot_neuron.reshape(pix_count, capacity), "pix", split_axis=0, concat_axis=0, tiled=True
    )
    asked_flat = asked_ids.reshape(slot_total)

    def slot_rows(source_rows):
        picked = source_rows[asked_flat].reshape(pix_count, capacity, source_rows.shape[1])
        returned = lax.all_to_all(picked, "pix", split_axis=0, concat_axis=0, tiled=True)
        return returned.reshape(slot_total, source_rows.shape[1])

    def residual_of(slot_traces):
        rebuilt = lax.dot_general(
            dense_map, slot_traces, (((0,), (0,)), ((), ())), preferred_element_type=jnp.float32
        )
        return (movie.astype(jnp.float32) - rebuilt).astype(jnp.bfloat16)

    slot_traces = slot_rows(traces)
    residual = residual_of(slot_traces)
    projection = jnp.dot(dense_map, residual, preferred_element_type=jnp.float32)
    slot_power = jnp.sum(masked.astype(jnp.float32) ** 2, axis=1)
    got_proj, got_power = (
        lax.all_to_all(
            projection.reshape(pix_count, capacity, projection.shape[1]),
            "pix",
            split_axis=0,
            concat_axis=0,
            tiled=True,
        ),
        lax.all_to_all(
            slot_power.reshape(pix_count, capacity), "pix", split_axis=0, concat_axis=0, tiled=True
        ),
    )
    owner_pick = (jnp.arange(neur_local, dtype=jnp.int32)[:, None] == asked_flat[None, :]).astype(
        jnp.float32
    )
    summed = jnp.dot(
        owner_pick,
        got_proj.reshape(slot_total, projection.shape[1]),
        precision=lax.Precision.HIGHEST,
    )
    power = jnp.dot(owner_pick, got_power.reshape(slot_total), precision=lax.Precision.HIGHEST)
    updated = jnp.maximum(
        0.0, traces.astype(jnp.float32) + summed / jnp.maximum(power, 0.5)[:, None]
    ).astype(jnp.bfloat16)
    slot_updated = slot_rows(updated)
    residual_two = residual_of(slot_updated)
    products = lax.dot_general(
        residual_two, slot_updated, (((1,), (1,)), ((), ())), preferred_element_type=jnp.float32
    )
    numerator = jnp.einsum(
        "bps,sb->sp",
        products.reshape(block_count, BLOCK, slot_total),
        block_pick.astype(jnp.float32),
        precision=lax.Precision.HIGHEST,
    )
    trace_power = jnp.sum(slot_updated.astype(jnp.float32) ** 2, axis=1)
    numer_all, power_all = lax.psum((numerator, trace_power), "tm")
    grown = jnp.maximum(0.0, masked.astype(jnp.float32) + numer_all / (power_all + 1e-06)[:, None])
    return (updated, jnp.where(usable[:, None], grown, 0.0))


def solution(mesh):
    return jax.shard_map(
        local,
        mesh=mesh,
        in_specs=(
            P("pix", "tm"),
            P("pix", "tm"),
            P("pix", None),
            P("pix"),
            P("pix"),
            P("pix", None),
        ),
        out_specs=(P("pix", "tm"), P("pix", None)),
        check_vma=False,
    )
```

profile of v0, /device:TPU:0, one launch (start us, length us, event | category | flops | bytes accessed | tf_op | source)
XLA Modules:
  0.0 106.1 jit_solution(13737110308454923679)
XLA Ops:
  7.2 1.4 %all_to_all.21 = s32[16,1,16]{2,1,0:T(1,128)} reshape(s32[256]{0:T(256)} %param.10) | data formatting | bytes 2048 | tf_op jit(solution)/shard_map/all_to_all | solution.py:26
  8.5 8.3 %all-to-all-start = ((s32[16,1,16]{2,1,0:T(1,128)}), s32[16,1,16]{2,1,0:T(1,128)S(1)}, u32[]{:S(2)}, u32[]{:S(2)}) async-start(s32[16,1,16]{2,1,0:T(1,128)} %all_to_all.21), calls=%async_computation | async-start | bytes 16384 | tf_op jit(solution)/shard_map/all_to_all | solution.py:26
  16.9 0.7 select_reduce_fusion
  17.6 1.0 fusion.17
  18.6 0.8 fusion.20
  19.4 0.7 all_to_all.25
  20.1 3.9 %all-to-all-done = s32[16,1,16]{2,1,0:T(1,128)S(1)} async-done(((s32[16,1,16]{2,1,0:T(1,128)}), s32[16,1,16]{2,1,0:T(1,128)S(1)}, u32[]{:S(2)}, u32[]{:S(2)}) %all-to-all-start) | async-done | bytes 1056 | tf_op jit(solution)/shard_map/all_to_all | solution.py:26
  24.0 0.1 reshape.146
  24.1 0.0 copy-start.2
  24.2 2.4 %gather_fusion = bf16[256,256]{1,0:T(8,128)(2,1)} fusion(bf16[32,256]{1,0:T(8,128)(2,1)} %param.7, s32[1024]{0:T(1024)S(1)} %pad_clamp_fusion), kind=kCustom, calls=%fused_computation | custom fusion | bytes 263168 | tf_op jit(solution)/shard_map/gather | solution.py:32
  26.6 3.5 %all-to-all-start.1 = ((bf16[16,16,256]{2,1,0:T(8,128)(2,1)}), bf16[16,16,256]{2,1,0:T(8,128)(2,1)S(1)}, u32[]{:S(2)}, u32[]{:S(2)}) async-start(bf16[16,16,256]{2,1,0:T(8,128)(2,1)} %bitcast.2), calls=%async_computation.1 | async-start | bytes 262144 | tf_op jit(solution)/shard_map/all_to_all | solution.py:33
  30.1 0.7 broadcast_multiply_fusion
  30.8 0.5 mul.44
  31.3 6.5 %all-to-all-done.1 = bf16[16,16,256]{2,1,0:T(8,128)(2,1)S(1)} async-done(((bf16[16,16,256]{2,1,0:T(8,128)(2,1)}), bf16[16,16,256]{2,1,0:T(8,128)(2,1)S(1)}, u32[]{:S(2)}, u32[]{:S(2)}) %all-to-all-start.1) | async-done | bytes 131104 | tf_op jit(solution)/shard_map/all_to_all | solution.py:33
  37.9 3.5 %all-to-all-start.3 = ((f32[16,1,16]{2,1,0:T(1,128)}), f32[16,1,16]{2,1,0:T(1,128)S(1)}, u32[]{:S(2)}, u32[]{:S(2)}) async-start(f32[16,1,16]{2,1,0:T(1,128)} %all_to_all.25), calls=%async_computation.3 | async-start | bytes 16384 | tf_op jit(solution)/shard_map/all_to_all | solution.py:54
  41.4 0.0 copy-done.2
  41.4 0.0 copy-start
  41.4 1.6 %fusion.10 = f32[16,16,256]{2,1,0:T(8,128)} fusion(bf16[16,16,2048]{2,1,0:T(8,128)(2,1)S(1)} %mul.44, bf16[256,256]{1,0:T(8,128)(2,1)S(1)} %bitcast.47, bf16[2048,256]{1,0:T(8,128)(2,1)S(1)} %copy-done.2, bf16[32,8,16,128]{3,2,1,0:T(8,128)(2,1)S(1)} %bitcast.39), kind=kOutput, calls=%fused_computation.15 | convolution fusion | flops 538443776 | bytes 3538944 | tf_op jit(solution)/shard_map/dot_general | solution.py:44
  43.0 5.6 %all-to-all-done.3 = f32[16,1,16]{2,1,0:T(1,128)S(1)} async-done(((f32[16,1,16]{2,1,0:T(1,128)}), f32[16,1,16]{2,1,0:T(1,128)S(1)}, u32[]{:S(2)}, u32[]{:S(2)}) %all-to-all-start.3) | async-done | bytes 1056 | tf_op jit(solution)/shard_map/all_to_all | solution.py:54
  48.6 3.5 %all-to-all-start.2 = ((f32[16,16,256]{2,1,0:T(8,128)}), f32[16,16,256]{2,1,0:T(8,128)S(1)}, u32[]{:S(2)}, u32[]{:S(2)}) async-start(f32[16,16,256]{2,1,0:T(8,128)} %fusion.10), calls=%async_computation.2 | async-start | bytes 524288 | tf_op jit(solution)/shard_map/all_to_all | solution.py:47
  52.1 0.0 all-reduce.2.cloned.1.call-start
  52.2 0.5 broadcast.122
  52.7 0.7 reduce.10
  53.4 0.1 eq.48
  53.5 0.5 broadcast.121
  54.0 0.7 reduce.9
  54.6 0.1 reshape.170
  54.7 0.1 fusion.6
  54.8 5.8 %all-to-all-done.2 = f32[16,16,256]{2,1,0:T(8,128)S(1)} async-done(((f32[16,16,256]{2,1,0:T(8,128)}), f32[16,16,256]{2,1,0:T(8,128)S(1)}, u32[]{:S(2)}, u32[]{:S(2)}) %all-to-all-start.2) | async-done | bytes 262176 | tf_op jit(solution)/shard_map/all_to_all | solution.py:47
  60.6 0.0 copy-done
  60.6 0.2 fusion.5
  60.8 0.0 copy-start.1
  60.8 1.2 %gather_fusion.1 = bf16[256,256]{1,0:T(8,128)(2,1)S(1)} fusion(bf16[32,256]{1,0:T(8,128)(2,1)S(1)} %fusion.5, s32[1024]{0:T(1024)S(1)} %pad_clamp_fusion), kind=kCustom, calls=%fused_computation.1 | custom fusion | bytes 263168 | tf_op jit(solution)/shard_map/gather | solution.py:32
  62.0 11.0 %all_to_all.33 = bf16[16,16,256]{2,1,0:T(8,128)(2,1)S(1)} all-to-all(bf16[16,16,256]{2,1,0:T(8,128)(2,1)S(1)} %bitcast.46), channel_id=1, replica_groups=mesh['pix'=16,'tm'=2] {'pix'}, dimensions={0} | all-to-all | bytes 262144 | tf_op jit(solution)/shard_map/all_to_all | solution.py:33
  73.1 0.6 fusion.1
  73.6 0.0 copy-done.1
  73.6 0.1 multiply_reduce_fusion
  73.7 0.1 reduce_sum.32
  73.8 2.4 %psum.15 = f32[256]{0:T(256)S(1)} all-reduce(f32[256]{0:T(256)S(1)} %reduce_sum.32), channel_id=1, replica_groups=mesh['pix'=16,'tm'=2] {'tm'}, use_global_device_ids=true, to_apply=%region_4.5 | all-reduce | flops 256 | bytes 2048 | tf_op jit(solution)/shard_map/psum | solution.py:82
  76.3 1.8 %fusion.28 = f32[16,128,256]{2,1,0:T(8,128)} fusion(bf16[16,128,256]{2,1,0:T(8,128)(2,1)S(1)} %bitcast.43, bf16[256,256,1]{1,0,2:T(8,128)(2,1)S(1)} %bitcast.42), kind=kOutput, calls=%fused_computation.47 | convolution fusion | flops 268435456 | bytes 3276800 | tf_op jit(solution)/shard_map/dot_general | solution.py:72
  78.1 2.2 %copy.8 = f32[16,128,256]{1,0,2:T(8,128)S(1)} copy(f32[16,128,256]{2,1,0:T(8,128)} %fusion.28) | data formatting | bytes 4194304 | tf_op jit(solution)/shard_map/dot_general | solution.py:72
  80.3 1.9 %fusion.15 = f32[256,1,128]{2,1,0:T(1,128)} fusion(f32[16,128,256]{1,0,2:T(8,128)S(1)} %copy.8, pred[256,16,1]{1,0,2:T(32,128)(4,1)S(1)} %get-tuple-element.6), kind=kOutput, calls=%fused_computation.19 | convolution fusion | flops 6291456 | bytes 2232320 | tf_op jit(solution)/shard_map/bps,sb->sp/dot_general | solution.py:75
  82.2 0.0 all-reduce.2.cloned.1.call-update
  82.3 15.3 %all-reduce.2.cloned.1.call-done = f32[256,128]{1,0:T(8,128)} async-done(((f32[256,128]{1,0:T(8,128)}), f32[256,128]{1,0:T(8,128)}) %all-reduce.2.cloned.1.call-update) | async-done | bytes 131088 | tf_op jit(solution)/shard_map/psum | solution.py:82
  97.5 1.7 %fusion.19 = f32[256,128]{1,0:T(8,128)} fusion(bf16[256,128]{1,0:T(8,128)(2,1)S(1)} %get-tuple-element.3, f32[256,128]{1,0:T(8,128)} %all-reduce.2.cloned.1.call-done, f32[256]{0:T(256)S(1)} %broadcast_add_fusion, pred[256]{0:T(512)(128)(4,1)S(1)} %get-tuple-element.5), kind=kLoop, calls=%fused_computation.26 | loop fusion | flops 163840 | bytes 328960 | tf_op jit(solution)/shard_map/jit(_where)/select_n | solution.py:84
  (5 shorter events, 0.0 us)
Async XLA Ops:
  8.5 15.5 %all-to-all-start = ((s32[16,1,16]{2,1,0:T(1,128)}), s32[16,1,16]{2,1,0:T(1,128)S(1)}, u32[]{:S(2)}, u32[]{:S(2)}) async-start(s32[16,1,16]{2,1,0:T(1,128)} %all_to_all.21), calls=%async_computation | async-start | bytes 16384 | tf_op jit(solution)/shard_map/all_to_all | solution.py:26
  24.1 17.2 %copy-start.2 = (bf16[2048,256]{1,0:T(8,128)(2,1)S(1)}, bf16[2048,256]{1,0:T(8,128)(2,1)}, u32[]{:S(2)}) copy-start(bf16[2048,256]{1,0:T(8,128)(2,1)} %param.6) | copy-start | bytes 3145732
  26.6 11.3 %all-to-all-start.1 = ((bf16[16,16,256]{2,1,0:T(8,128)(2,1)}), bf16[16,16,256]{2,1,0:T(8,128)(2,1)S(1)}, u32[]{:S(2)}, u32[]{:S(2)}) async-start(bf16[16,16,256]{2,1,0:T(8,128)(2,1)} %bitcast.2), calls=%async_computation.1 | async-start | bytes 262144 | tf_op jit(solution)/shard_map/all_to_all | solution.py:33
  37.9 10.7 %all-to-all-start.3 = ((f32[16,1,16]{2,1,0:T(1,128)}), f32[16,1,16]{2,1,0:T(1,128)S(1)}, u32[]{:S(2)}, u32[]{:S(2)}) async-start(f32[16,1,16]{2,1,0:T(1,128)} %all_to_all.25), calls=%async_computation.3 | async-start | bytes 16384 | tf_op jit(solution)/shard_map/all_to_all | solution.py:54
  41.4 19.2 %copy-start = (bf16[32,256]{1,0:T(8,128)(2,1)S(1)}, bf16[32,256]{1,0:T(8,128)(2,1)}, u32[]{:S(2)}) copy-start(bf16[32,256]{1,0:T(8,128)(2,1)} %param.7) | copy-start | bytes 49156
  48.6 12.0 %all-to-all-start.2 = ((f32[16,16,256]{2,1,0:T(8,128)}), f32[16,16,256]{2,1,0:T(8,128)S(1)}, u32[]{:S(2)}, u32[]{:S(2)}) async-start(f32[16,16,256]{2,1,0:T(8,128)} %fusion.10), calls=%async_computation.2 | async-start | bytes 524288 | tf_op jit(solution)/shard_map/all_to_all | solution.py:47
  52.1 45.4 %all-reduce.2.cloned.1.call-start = ((), (), s32[]{:S(2)}) async-start(), calls=%async_computation.5 | async-start | bytes 262144 | tf_op jit(solution)/shard_map/psum | solution.py:82
  60.8 12.8 %copy-start.1 = (bf16[32,256]{1,0:T(8,128)(2,1)}, bf16[32,256]{1,0:T(8,128)(2,1)S(1)}, u32[]{:S(2)}) copy-start(bf16[32,256]{1,0:T(8,128)(2,1)S(1)} %fusion.5) | copy-start | bytes 49156
Sparse Core Ops, SparseCore 0:
  82.4 15.1 all-reduce.1
where the time goes:
time: 107 us; the launch traced here: 106 us
  waiting for transfers between devices  37.1 us (35%)
  starting transfers between devices  18.9 us (18%)
  between operations  14.2 us (13%)
  blocking collectives  13.5 us (13%)
  local copies, waits for them, and re-layouts  9.73 us (9%)
  other arithmetic  6.42 us (6%)
  matrix products  6.23 us (6%)
    psum x1, waiting for transfers between devices, local(): numer_all, power_all = lax.psum((numerator, trace_power), 'tm')  15.3 us
    all_to_all x1, blocking collectives, slot_rows(): lax.all_to_all(picked, 'pix', split_axis=0, concat_axis=0, tiled=True)  11 us
    all_to_all x1, starting transfers between devices, local(): lax.all_to_all(slot_neuron.reshape(pix_count, capacity), 'pix', split_axi...  8.31 us
    all_to_all x1, waiting for transfers between devices, slot_rows(): lax.all_to_all(picked, 'pix', split_axis=0, concat_axis=0, tiled=True)  6.55 us
    all_to_all x1, waiting for transfers between devices, local(): lax.all_to_all(projection.reshape(pix_count, capacity, projection.shape[1...  5.76 us
    all_to_all x1, waiting for transfers between devices, local(): lax.all_to_all(slot_power.reshape(pix_count, capacity), 'pix', split_axis...  5.58 us
    all_to_all x1, waiting for transfers between devices, local(): lax.all_to_all(slot_neuron.reshape(pix_count, capacity), 'pix', split_axi...  3.94 us
    gather x2, local copies, waits for them, and re-layouts, slot_rows(): source_rows[asked_flat].reshape(pix_count, capacity, source_rows.shape[1])  3.58 us
  transfers between devices with their start and end apart: 5, of which 5 were waited for; matrix products, arithmetic and copies ran while one was open for 8% of the time, Pallas kernels for 0%

commit v1 on v0

v1 whole, which is shorter than its diff:
```python
import functools

import jax
import jax.numpy as jnp
from jax import lax
from jax.experimental import pallas as pl
from jax.experimental.pallas import tpu as pltpu
from jax.sharding import PartitionSpec as P

BLOCK = 128
ROWS = 16
SIDE = 128
F32 = jnp.float32
BF16 = jnp.bfloat16
NN = (((1,), (0,)), ((), ()))
NT = (((1,), (1,)), ((), ()))
TN = (((0,), (0,)), ((), ()))


def dot(a, b, dims=NN):
    return lax.dot_general(a, b, dims, preferred_element_type=F32)


def split(value):
    high = value.astype(BF16)
    return high, (value - high.astype(F32)).astype(BF16)


def iota(shape, dim):
    return lax.broadcasted_iota(jnp.int32, shape, dim)


def near_order(n):
    return sorted(range(1, n), key=lambda k: (abs(k - n // 2), k))


def kernel(
    n, t, movie_hbm, traces_hbm, foot_hbm, block_hbm, neuron_hbm, fill_hbm,
    new_ref, grown_ref,
    movie, foot, block_ref, neuron_ref, fill_ref,
    all_traces, proj_out, proj_in, back_out, back_in, num_out, num_in, pow_out, pow_in,
    local_sem, send_sem, recv_sem, tm_send, tm_recv,
):
    me = lax.axis_index("pix")
    core = lax.axis_index("tm")
    slots = foot.shape[0]
    cap = slots // n
    neur = traces_hbm.shape[0]
    frames = movie.shape[1]
    blocks = movie.shape[0] // BLOCK
    neurons = n * neur

    def pix_id(peer):
        return (peer, core)

    def peers(body):
        if n <= 16:
            for k in near_order(n):
                body(lax.rem(me + k, n))
        else:
            lax.fori_loop(1, n, lambda k, _: (body(lax.rem(me + k, n)), 0)[1], 0)

    def part(index, size):
        return pl.ds(pl.multiple_of(index * size, size), size)

    barrier = pltpu.get_barrier_semaphore()
    peers(lambda p: pl.semaphore_signal(barrier, inc=1, device_id=pix_id(p)))
    for k in range(1, t):
        pl.semaphore_signal(barrier, inc=1, device_id=(me, lax.rem(core + k, t)))

    mine = all_traces.at[part(me, neur)]
    loads = [
        pltpu.make_async_copy(a, b, local_sem.at[i])
        for i, (a, b) in enumerate(
            [
                (traces_hbm, mine),
                (foot_hbm, foot),
                (block_hbm, block_ref),
                (neuron_hbm, neuron_ref),
                (fill_hbm, fill_ref),
                (movie_hbm, movie),
            ]
        )
    ]
    for load in loads:
        load.start()
    loads[0].wait()
    pl.semaphore_wait(barrier, n - 1 + t - 1)

    def trace_copy(p, source):
        return pltpu.make_async_remote_copy(
            src_ref=mine,
            dst_ref=all_traces.at[part(source, neur)],
            send_sem=send_sem.at[0, p],
            recv_sem=recv_sem.at[0, source],
            device_id=pix_id(p),
        )

    peers(lambda p: trace_copy(p, me).start())
    for load in loads[1:5]:
        load.wait()

    diag = iota((slots, slots), 0) == iota((slots, slots), 1)

    def column(row):
        return jnp.sum(jnp.where(diag, row.astype(F32), 0.0), axis=1, keepdims=True)

    block_row = block_ref[...].astype(F32)
    block_col = column(block_row)
    neuron_col = column(neuron_ref[...])
    owner_hit = lax.div(iota((slots, n), 0), cap) == iota((slots, n), 1)
    fill_col = jnp.sum(jnp.where(owner_hit, fill_ref[...].astype(F32), 0.0), axis=1, keepdims=True)
    row_of = iota((slots, 1), 0)
    usable = lax.rem(row_of, cap).astype(F32) < fill_col
    masked = jnp.where(usable, foot[...].astype(F32), 0.0)
    masked_b = masked.astype(BF16)
    same_block = block_col == block_row
    power = jnp.sum(masked * masked, axis=1, keepdims=True)
    lane = iota((slots, SIDE), 1)
    power_high, rest = split(power)
    power_mid, power_low = split(power - power_high.astype(F32))
    side = jnp.where(
        lane == 0,
        neuron_col,
        jnp.where(
            lane == 1,
            power_high.astype(F32),
            jnp.where(
                lane == 2,
                power_mid.astype(F32),
                jnp.where(lane == 3, power_low.astype(F32), 0.0),
            ),
        ),
    ).astype(BF16)

    padded = n * ROWS
    if cap == ROWS:
        widen = narrow = lambda x: x
    else:
        slot_row = lax.div(iota((padded, slots), 0), ROWS) * cap + lax.rem(
            iota((padded, slots), 0), ROWS
        )
        real = lax.rem(iota((padded, slots), 0), ROWS) < cap
        place = ((slot_row == iota((padded, slots), 1)) & real).astype(BF16)

        def widen(x):
            return dot(place, x).astype(BF16)

        def narrow(x):
            return dot(place, x, TN).astype(BF16)

    proj_out[:, frames:] = widen(side)

    gram = jnp.where(same_block, dot(masked_b, masked_b, NT), 0.0)
    neuron_id = lax.div(row_of, cap).astype(F32) * neur + neuron_col
    pick = (neuron_id == iota((slots, neurons), 1).astype(F32)).astype(BF16)
    gram_high, gram_low = split(gram)
    couple_high, couple_low = split(dot(gram_high, pick) + dot(gram_low, pick))

    loads[5].wait()
    base = jnp.zeros((slots, frames), F32)
    for b in range(0, blocks, 2):
        pair = jnp.concatenate(
            [jnp.where(block_col == float(b + j), masked, 0.0).astype(BF16) for j in range(2)],
            axis=1,
        )
        base += dot(pair, movie[b * BLOCK : (b + 2) * BLOCK, :])

    peers(lambda p: trace_copy(p, p).wait_recv())
    gathered = all_traces[...]
    projection = base - (dot(couple_high, gathered) + dot(couple_low, gathered))
    proj_out[:, :frames] = widen(projection.astype(BF16))

    def proj_copy(p, source):
        return pltpu.make_async_remote_copy(
            src_ref=proj_out.at[part(p, ROWS)],
            dst_ref=proj_in.at[part(source, ROWS)],
            send_sem=send_sem.at[1, p],
            recv_sem=recv_sem.at[1, source],
            device_id=pix_id(p),
        )

    peers(lambda p: proj_copy(p, me).start())
    proj_in[part(me, ROWS), :] = proj_out[part(me, ROWS), :]
    peers(lambda p: proj_copy(p, p).wait_recv())

    got = proj_in[...]
    asked = got[:, frames : frames + 1].astype(F32)
    owner_pick = asked == iota((padded, neur), 1).astype(F32)
    if cap != ROWS:
        owner_pick &= lax.rem(iota((padded, neur), 0), ROWS) < cap
    owner_pick = owner_pick.astype(F32).astype(BF16)
    sums = dot(owner_pick, got, TN)
    total_power = (
        sums[:, frames + 1 : frames + 2]
        + sums[:, frames + 2 : frames + 3]
        + sums[:, frames + 3 : frames + 4]
    )
    own = all_traces[part(me, neur), :].astype(F32)
    updated = jnp.maximum(0.0, own + sums[:, :frames] / jnp.maximum(total_power, 0.5)).astype(BF16)
    new_ref[...] = updated
    back_out[...] = dot(owner_pick, updated).astype(BF16)

    def back_copy(p, source):
        return pltpu.make_async_remote_copy(
            src_ref=back_out.at[part(p, ROWS)],
            dst_ref=back_in.at[part(source, ROWS)],
            send_sem=send_sem.at[2, p],
            recv_sem=recv_sem.at[2, source],
            device_id=pix_id(p),
        )

    peers(lambda p: back_copy(p, me).start())
    back_in[part(me, ROWS), :] = back_out[part(me, ROWS), :]
    peers(lambda p: back_copy(p, p).wait_recv())

    fresh = narrow(back_in[...])
    fresh_f = fresh.astype(F32)
    pow_out[...] = jnp.broadcast_to(
        jnp.sum(fresh_f * fresh_f, axis=1, keepdims=True), (slots, BLOCK)
    )

    def tm_copy(index, out, into, q, source):
        return pltpu.make_async_remote_copy(
            src_ref=out,
            dst_ref=into.at[source],
            send_sem=tm_send.at[index, q],
            recv_sem=tm_recv.at[index, source],
            device_id=(me, q),
        )

    partners = [lax.rem(core + k, t) for k in range(1, t)]
    for q in partners:
        tm_copy(0, pow_out, pow_in, q, core).start()
    overlap = jnp.where(same_block, dot(fresh, fresh, NT), 0.0)
    over_high, over_low = split(overlap)
    numerator = -(dot(over_high, masked_b) + dot(over_low, masked_b))
    for b in range(0, blocks, 2):
        product = dot(fresh, movie[b * BLOCK : (b + 2) * BLOCK, :], NT)
        for j in range(2):
            numerator += jnp.where(
                block_col == float(b + j), product[:, j * BLOCK : (j + 1) * BLOCK], 0.0
            )
    num_out[...] = numerator
    for q in partners:
        tm_copy(1, num_out, num_in, q, core).start()
    pow_in[core] = pow_out[...]
    num_in[core] = numerator
    for q in partners:
        tm_copy(0, pow_out, pow_in, q, q).wait_recv()
        tm_copy(1, num_out, num_in, q, q).wait_recv()
    num_all, pow_all = num_in[0], pow_in[0]
    for q in range(1, t):
        num_all += num_in[q]
        pow_all += pow_in[q]
    grown = jnp.maximum(0.0, masked + num_all / (pow_all + 1e-06))
    grown_ref[...] = jnp.where(usable, grown, 0.0)

    peers(lambda p: trace_copy(p, me).wait_send())
    peers(lambda p: proj_copy(p, me).wait_send())
    peers(lambda p: back_copy(p, me).wait_send())
    for q in partners:
        tm_copy(0, pow_out, pow_in, q, core).wait_send()
        tm_copy(1, num_out, num_in, q, core).wait_send()


def local(n, t, movie, traces, footprints, slot_block, slot_neuron, bucket_fill):
    slots = footprints.shape[0]
    neur, frames = traces.shape
    padded = n * ROWS
    return pl.pallas_call(
        functools.partial(kernel, n, t),
        out_shape=(
            jax.ShapeDtypeStruct((neur, frames), BF16),
            jax.ShapeDtypeStruct((slots, BLOCK), F32),
        ),
        in_specs=[pl.BlockSpec(memory_space=pl.ANY)] * 6,
        out_specs=[pl.BlockSpec(memory_space=pltpu.VMEM)] * 2,
        scratch_shapes=[
            pltpu.VMEM(movie.shape, BF16),
            pltpu.VMEM(footprints.shape, BF16),
            pltpu.VMEM((1, slots), jnp.int32),
            pltpu.VMEM((1, slots), jnp.int32),
            pltpu.VMEM((1, n), jnp.int32),
            pltpu.VMEM((n * neur, frames), BF16),
            pltpu.VMEM((padded, frames + SIDE), BF16),
            pltpu.VMEM((padded, frames + SIDE), BF16),
            pltpu.VMEM((padded, frames), BF16),
            pltpu.VMEM((padded, frames), BF16),
            pltpu.VMEM((slots, BLOCK), F32),
            pltpu.VMEM((t, slots, BLOCK), F32),
            pltpu.VMEM((slots, BLOCK), F32),
            pltpu.VMEM((t, slots, BLOCK), F32),
            pltpu.SemaphoreType.DMA((6,)),
            pltpu.SemaphoreType.DMA((3, n)),
            pltpu.SemaphoreType.DMA((3, n)),
            pltpu.SemaphoreType.DMA((2, t)),
            pltpu.SemaphoreType.DMA((2, t)),
        ],
        compiler_params=pltpu.CompilerParams(
            collective_id=0, has_side_effects=True, vmem_limit_bytes=48 * 1024 * 1024
        ),
    )(
        movie,
        traces,
        footprints,
        slot_block.reshape(1, slots),
        slot_neuron.reshape(1, slots),
        bucket_fill,
    )


def solution(mesh):
    return jax.shard_map(
        functools.partial(local, mesh.shape["pix"], mesh.shape["tm"]),
        mesh=mesh,
        in_specs=(
            P("pix", "tm"),
            P("pix", "tm"),
            P("pix", None),
            P("pix"),
            P("pix"),
            P("pix", None),
        ),
        out_specs=(P("pix", "tm"), P("pix", None)),
        check_vma=False,
    )
```

time: 107 us -> 34.1 us (0.32)
  waiting for transfers between devices: 37.1 us -> 0 us
  Pallas kernels: 0 us -> 28.4 us
  starting transfers between devices: 18.9 us -> 0 us
  between operations: 14.2 us -> 0.67 us
  blocking collectives: 13.5 us -> 0 us
  other arithmetic: 6.42 us -> 0 us
  matrix products: 6.23 us -> 0 us
  local copies, waits for them, and re-layouts: 9.73 us -> 4.72 us
    pallas_call x0 -> x1, Pallas kernels: none -> 28.4 us  [local(): pl.pallas_call(functools.partial(kernel, n, t), out_shape=(jax.ShapeDtype...]
    all_to_all x4 -> x0, waiting for transfers between devices: 21.8 us -> none  [the longest x1 6.55 us: slot_rows(): lax.all_to_all(picked, 'pix', split_axis=0, concat_axis=0, tiled=True)]
    all_to_all x4 -> x0, starting transfers between devices: 18.8 us -> none  [the longest x1 8.31 us: local(): lax.all_to_all(slot_neuron.reshape(pix_count, capacity), 'pix', split_axi...]
    psum x1 -> x0, waiting for transfers between devices: 15.3 us -> none  [local(): numer_all, power_all = lax.psum((numerator, trace_power), 'tm')]
    all_to_all x1 -> x0, blocking collectives: 11 us -> none  [slot_rows(): lax.all_to_all(picked, 'pix', split_axis=0, concat_axis=0, tiled=True)]
    dot_general x6 -> x0, matrix products: 6.23 us -> none  [the longest x1 1.88 us: local(): jnp.einsum('bps,sb->sp', products.reshape(block_count, BLOCK, slot_total)...]
    unnamed x6 -> x14, local copies, waits for them, and re-layouts: 0.02 us -> 4.72 us
    gather x2 -> x0, local copies, waits for them, and re-layouts: 3.58 us -> none  [slot_rows(): source_rows[asked_flat].reshape(pix_count, capacity, source_rows.shape[1])]
  transfers between devices with their start and end apart: 5 -> 0, of which waited for: 5 -> 0; matrix products, arithmetic and copies ran while one was open for 8% -> 0% of each run, Pallas kernels for 0% -> 0%
where the time goes in v1:
time: 34.1 us; the launch traced here: 33.8 us
  Pallas kernels  28.4 us (83%)
  local copies, waits for them, and re-layouts  4.72 us (14%)
  between operations  0.67 us (2%)
    pallas_call x1, Pallas kernels, local(): pl.pallas_call(functools.partial(kernel, n, t), out_shape=(jax.ShapeDtype...  28.4 us
    unnamed x14, local copies, waits for them, and re-layouts  4.72 us

profile of v1, /device:TPU:0, one launch (start us, length us, event | category | flops | bytes accessed | tf_op | source)
XLA Modules:
  0.0 33.8 jit_solution(11562217622055555275)
XLA Ops:
  0.6 0.0 copy-start.4
  0.6 0.0 copy-start.3
  0.7 0.0 copy-start.5
  0.7 0.7 %copy-done.4 = s32[256]{0:T(256)S(1)} copy-done((s32[256]{0:T(256)S(1)}, s32[256]{0:T(256)}, u32[]{:S(2)}) %copy-start.4) | copy-done | bytes 1048
  1.3 0.0 copy-done.3
  1.3 0.0 copy-done.5
  1.3 0.0 copy-start
  1.3 1.2 %copy-done = bf16[2048,256]{1,0:T(8,128)(2,1)S(1)} copy-done((bf16[2048,256]{1,0:T(8,128)(2,1)S(1)}, bf16[2048,256]{1,0:T(8,128)(2,1)}, u32[]{:S(2)}) %copy-start) | copy-done | bytes 1048600
  2.6 0.0 copy-start.1
  2.6 0.8 %copy-done.1 = bf16[256,128]{1,0:T(8,128)(2,1)S(1)} copy-done((bf16[256,128]{1,0:T(8,128)(2,1)S(1)}, bf16[256,128]{1,0:T(8,128)(2,1)}, u32[]{:S(2)}) %copy-start.1) | copy-done | bytes 65560
  3.4 0.0 copy-start.2
  3.4 0.7 %copy-done.2 = bf16[32,256]{1,0:T(8,128)(2,1)S(1)} copy-done((bf16[32,256]{1,0:T(8,128)(2,1)S(1)}, bf16[32,256]{1,0:T(8,128)(2,1)}, u32[]{:S(2)}) %copy-start.2) | copy-done | bytes 16408
  4.1 28.4 %shard_map.77 = (bf16[32,256]{1,0:T(8,128)(2,1)S(1)}, f32[256,128]{1,0:T(8,128)S(1)}) custom-call(bf16[2048,256]{1,0:T(8,128)(2,1)S(1)} %copy-done, bf16[32,256]{1,0:T(8,128)(2,1)S(1)} %copy-done.2, bf16[256,128]{1,0:T(8,128)(2,1)S(1)} %copy-done.1, s32[1,256]{1,0:T(1,128)S(1)} %bitcast.2, s32[1,256]{1,0:T(1,128)S(1)} %bitcast.3, s32[1,16]{1,0:T(1,128)S(1)} %copy-done.5), custom_call_target="tpu_custom_call" | custom-call | tf_op jit(solution)/shard_map/pallas_call | solution.py:271
  32.5 0.6 %copy.10 = bf16[32,256]{1,0:T(8,128)(2,1)} copy(bf16[32,256]{1,0:T(8,128)(2,1)S(1)} %get-tuple-element.4) | data formatting | bytes 32768
  33.2 0.7 %copy.11 = f32[256,128]{1,0:T(8,128)} copy(f32[256,128]{1,0:T(8,128)S(1)} %get-tuple-element.5) | data formatting | bytes 262144
Async XLA Ops:
  0.6 0.7 %copy-start.4 = (s32[256]{0:T(256)S(1)}, s32[256]{0:T(256)}, u32[]{:S(2)}) copy-start(s32[256]{0:T(256)} %param.10) | copy-start | bytes 3076
  0.6 0.7 %copy-start.3 = (s32[256]{0:T(256)S(1)}, s32[256]{0:T(256)}, u32[]{:S(2)}) copy-start(s32[256]{0:T(256)} %param.9) | copy-start | bytes 3076
  0.7 0.7 %copy-start.5 = (s32[1,16]{1,0:T(1,128)S(1)}, s32[1,16]{1,0:T(1,128)}, u32[]{:S(2)}) copy-start(s32[1,16]{1,0:T(1,128)} %fill_hbm.1) | copy-start | bytes 196
  1.3 1.2 %copy-start = (bf16[2048,256]{1,0:T(8,128)(2,1)S(1)}, bf16[2048,256]{1,0:T(8,128)(2,1)}, u32[]{:S(2)}) copy-start(bf16[2048,256]{1,0:T(8,128)(2,1)} %movie_hbm.1) | copy-start | bytes 3145732
  2.6 0.8 %copy-start.1 = (bf16[256,128]{1,0:T(8,128)(2,1)S(1)}, bf16[256,128]{1,0:T(8,128)(2,1)}, u32[]{:S(2)}) copy-start(bf16[256,128]{1,0:T(8,128)(2,1)} %foot_hbm.1) | copy-start | bytes 196612
  3.4 0.7 %copy-start.2 = (bf16[32,256]{1,0:T(8,128)(2,1)S(1)}, bf16[32,256]{1,0:T(8,128)(2,1)}, u32[]{:S(2)}) copy-start(bf16[32,256]{1,0:T(8,128)(2,1)} %traces_hbm.1) | copy-start | bytes 49156

commit v2 on v1

--- a/solution.py
+++ b/solution.py
@@ -9,7 +9,8 @@
 
 BLOCK = 128
 ROWS = 16
-SIDE = 128
+LANES = 128
+PARTS = 1
 F32 = jnp.float32
 BF16 = jnp.bfloat16
 NN = (((1,), (0,)), ((), ()))
@@ -26,6 +27,12 @@
     return high, (value - high.astype(F32)).astype(BF16)
 
 
+def exact_dot(ones, b):
+    high, rest = b.astype(BF16), b - b.astype(BF16).astype(F32)
+    mid, low = split(rest)
+    return dot(ones, high) + dot(ones, mid) + dot(ones, low)
+
+
 def iota(shape, dim):
     return lax.broadcasted_iota(jnp.int32, shape, dim)
 
@@ -38,8 +45,9 @@
     n, t, movie_hbm, traces_hbm, foot_hbm, block_hbm, neuron_hbm, fill_hbm,
     new_ref, grown_ref,
     movie, foot, block_ref, neuron_ref, fill_ref,
-    all_traces, proj_out, proj_in, back_out, back_in, num_out, num_in, pow_out, pow_in,
-    local_sem, send_sem, recv_sem, tm_send, tm_recv,
+    all_traces, side_out, side_in, proj_out, proj_in, back_out, back_in,
+    num_out, num_in, pow_out, pow_in,
+    local_sem, send_sem, recv_sem, side_send, side_recv, tm_send, tm_recv,
 ):
     me = lax.axis_index("pix")
     core = lax.axis_index("tm")
@@ -49,6 +57,8 @@
     frames = movie.shape[1]
     blocks = movie.shape[0] // BLOCK
     neurons = n * neur
+    wide = frames // PARTS
+    pieces = range(PARTS)
 
     def pix_id(peer):
         return (peer, core)
@@ -68,12 +78,17 @@
     for k in range(1, t):
         pl.semaphore_signal(barrier, inc=1, device_id=(me, lax.rem(core + k, t)))
 
-    mine = all_traces.at[part(me, neur)]
+    def mine(h):
+        return all_traces.at[h, part(me, neur)]
+
+    def strip(h):
+        return slice(h * wide, (h + 1) * wide)
+
     loads = [
         pltpu.make_async_copy(a, b, local_sem.at[i])
         for i, (a, b) in enumerate(
-            [
-                (traces_hbm, mine),
+            [(traces_hbm.at[:, pl.ds(h * wide, wide)], mine(h)) for h in pieces]
+            + [
                 (foot_hbm, foot),
                 (block_hbm, block_ref),
                 (neuron_hbm, neuron_ref),
@@ -84,20 +99,22 @@
     ]
     for load in loads:
         load.start()
-    loads[0].wait()
+    for h in pieces:
+        loads[h].wait()
     pl.semaphore_wait(barrier, n - 1 + t - 1)
 
-    def trace_copy(p, source):
-        return pltpu.make_async_remote_copy(
-            src_ref=mine,
-            dst_ref=all_traces.at[part(source, neur)],
-            send_sem=send_sem.at[0, p],
-            recv_sem=recv_sem.at[0, source],
+    def trace_copy(h, p, source):
+        return pltpu.make_async_remote_copy(
+            src_ref=mine(h),
+            dst_ref=all_traces.at[h, part(source, neur)],
+            send_sem=send_sem.at[0, h, p],
+            recv_sem=recv_sem.at[0, h, source],
             device_id=pix_id(p),
         )
 
-    peers(lambda p: trace_copy(p, me).start())
-    for load in loads[1:5]:
+    for h in pieces:
+        peers(lambda p: trace_copy(h, p, me).start())
+    for load in loads[PARTS:-1]:
         load.wait()
 
     diag = iota((slots, slots), 0) == iota((slots, slots), 1)
@@ -116,22 +133,27 @@
     masked_b = masked.astype(BF16)
     same_block = block_col == block_row
     power = jnp.sum(masked * masked, axis=1, keepdims=True)
-    lane = iota((slots, SIDE), 1)
-    power_high, rest = split(power)
-    power_mid, power_low = split(power - power_high.astype(F32))
+    lane = iota((slots, LANES), 1)
+    place_of = lax.rem(row_of, cap)
     side = jnp.where(
-        lane == 0,
-        neuron_col,
-        jnp.where(
-            lane == 1,
-            power_high.astype(F32),
-            jnp.where(
-                lane == 2,
-                power_mid.astype(F32),
-                jnp.where(lane == 3, power_low.astype(F32), 0.0),
-            ),
-        ),
-    ).astype(BF16)
+        lane == place_of, neuron_col, jnp.where(lane == place_of + ROWS, power, 0.0)
+    )
+    to_owner = (lax.div(iota((n, slots), 1), cap) == iota((n, slots), 0)).astype(BF16)
+    side = exact_dot(to_owner, side)
+    for o in range(n):
+        side_out[o] = side[o : o + 1, :]
+
+    def side_copy(p, source):
+        return pltpu.make_async_remote_copy(
+            src_ref=side_out.at[p],
+            dst_ref=side_in.at[source],
+            send_sem=side_send.at[p],
+            recv_sem=side_recv.at[source],
+            device_id=pix_id(p),
+        )
+
+    peers(lambda p: side_copy(p, me).start())
+    side_in[me] = side_out[me]
 
     padded = n * ROWS
     if cap == ROWS:
@@ -149,15 +171,13 @@
         def narrow(x):
             return dot(place, x, TN).astype(BF16)
 
-    proj_out[:, frames:] = widen(side)
-
     gram = jnp.where(same_block, dot(masked_b, masked_b, NT), 0.0)
     neuron_id = lax.div(row_of, cap).astype(F32) * neur + neuron_col
     pick = (neuron_id == iota((slots, neurons), 1).astype(F32)).astype(BF16)
     gram_high, gram_low = split(gram)
     couple_high, couple_low = split(dot(gram_high, pick) + dot(gram_low, pick))
 
-    loads[5].wait()
+    loads[-1].wait()
     base = jnp.zeros((slots, frames), F32)
     for b in range(0, blocks, 2):
         pair = jnp.concatenate(
@@ -166,55 +186,63 @@
         )
         base += dot(pair, movie[b * BLOCK : (b + 2) * BLOCK, :])
 
-    peers(lambda p: trace_copy(p, p).wait_recv())
-    gathered = all_traces[...]
-    projection = base - (dot(couple_high, gathered) + dot(couple_low, gathered))
-    proj_out[:, :frames] = widen(projection.astype(BF16))
-
-    def proj_copy(p, source):
-        return pltpu.make_async_remote_copy(
-            src_ref=proj_out.at[part(p, ROWS)],
-            dst_ref=proj_in.at[part(source, ROWS)],
-            send_sem=send_sem.at[1, p],
-            recv_sem=recv_sem.at[1, source],
+    def proj_copy(h, p, source):
+        return pltpu.make_async_remote_copy(
+            src_ref=proj_out.at[h, part(p, ROWS)],
+            dst_ref=proj_in.at[h, part(source, ROWS)],
+            send_sem=send_sem.at[1, h, p],
+            recv_sem=recv_sem.at[1, h, source],
             device_id=pix_id(p),
         )
 
-    peers(lambda p: proj_copy(p, me).start())
-    proj_in[part(me, ROWS), :] = proj_out[part(me, ROWS), :]
-    peers(lambda p: proj_copy(p, p).wait_recv())
-
-    got = proj_in[...]
-    asked = got[:, frames : frames + 1].astype(F32)
-    owner_pick = asked == iota((padded, neur), 1).astype(F32)
+    for h in pieces:
+        peers(lambda p: trace_copy(h, p, p).wait_recv())
+        gathered = all_traces[h]
+        projection = base[:, strip(h)] - (dot(couple_high, gathered) + dot(couple_low, gathered))
+        proj_out[h] = widen(projection.astype(BF16))
+        peers(lambda p: proj_copy(h, p, me).start())
+        proj_in[h, part(me, ROWS), :] = proj_out[h, part(me, ROWS), :]
+
+    peers(lambda p: side_copy(p, p).wait_recv())
+    side_rows = jnp.concatenate([side_in[i] for i in range(n)], axis=0)
+    from_tile = (lax.div(iota((padded, n), 0), ROWS) == iota((padded, n), 1)).astype(BF16)
+    spread = exact_dot(from_tile, side_rows)
+    spread_lane = iota((padded, LANES), 1)
+    spread_place = lax.rem(iota((padded, 1), 0), ROWS)
+    asked = jnp.sum(jnp.where(spread_lane == spread_place, spread, 0.0), axis=1, keepdims=True)
+    asked_power = jnp.sum(
+        jnp.where(spread_lane == spread_place + ROWS, spread, 0.0), axis=1, keepdims=True
+    )
+    hit = asked == iota((padded, neur), 1).astype(F32)
     if cap != ROWS:
-        owner_pick &= lax.rem(iota((padded, neur), 0), ROWS) < cap
-    owner_pick = owner_pick.astype(F32).astype(BF16)
-    sums = dot(owner_pick, got, TN)
-    total_power = (
-        sums[:, frames + 1 : frames + 2]
-        + sums[:, frames + 2 : frames + 3]
-        + sums[:, frames + 3 : frames + 4]
-    )
-    own = all_traces[part(me, neur), :].astype(F32)
-    updated = jnp.maximum(0.0, own + sums[:, :frames] / jnp.maximum(total_power, 0.5)).astype(BF16)
-    new_ref[...] = updated
-    back_out[...] = dot(owner_pick, updated).astype(BF16)
-
-    def back_copy(p, source):
-        return pltpu.make_async_remote_copy(
-            src_ref=back_out.at[part(p, ROWS)],
-            dst_ref=back_in.at[part(source, ROWS)],
-            send_sem=send_sem.at[2, p],
-            recv_sem=recv_sem.at[2, source],
+        hit &= lax.rem(iota((padded, neur), 0), ROWS) < cap
+    owner_pick = hit.astype(F32).astype(BF16)
+    pick_turned = jnp.transpose(hit.astype(F32)).astype(BF16)
+    total_power = exact_dot(pick_turned, jnp.broadcast_to(asked_power, (padded, LANES)))[:, 0:1]
+    floor_power = jnp.maximum(total_power, 0.5)
+
+    def back_copy(h, p, source):
+        return pltpu.make_async_remote_copy(
+            src_ref=back_out.at[h, part(p, ROWS)],
+            dst_ref=back_in.at[h, part(source, ROWS)],
+            send_sem=send_sem.at[2, h, p],
+            recv_sem=recv_sem.at[2, h, source],
             device_id=pix_id(p),
         )
 
-    peers(lambda p: back_copy(p, me).start())
-    back_in[part(me, ROWS), :] = back_out[part(me, ROWS), :]
-    peers(lambda p: back_copy(p, p).wait_recv())
-
-    fresh = narrow(back_in[...])
+    for h in pieces:
+        peers(lambda p: proj_copy(h, p, p).wait_recv())
+        own = all_traces[h, part(me, neur), :].astype(F32)
+        sums = dot(pick_turned, proj_in[h])
+        updated = jnp.maximum(0.0, own + sums / floor_power).astype(BF16)
+        back_out[h] = dot(owner_pick, updated).astype(BF16)
+        peers(lambda p: back_copy(h, p, me).start())
+        back_in[h, part(me, ROWS), :] = back_out[h, part(me, ROWS), :]
+        new_ref[:, strip(h)] = updated
+
+    for h in pieces:
+        peers(lambda p: back_copy(h, p, p).wait_recv())
+    fresh = jnp.concatenate([narrow(back_in[h]) for h in pieces], axis=1)
     fresh_f = fresh.astype(F32)
     pow_out[...] = jnp.broadcast_to(
         jnp.sum(fresh_f * fresh_f, axis=1, keepdims=True), (slots, BLOCK)
@@ -256,9 +284,11 @@
     grown = jnp.maximum(0.0, masked + num_all / (pow_all + 1e-06))
     grown_ref[...] = jnp.where(usable, grown, 0.0)
 
-    peers(lambda p: trace_copy(p, me).wait_send())
-    peers(lambda p: proj_copy(p, me).wait_send())
-    peers(lambda p: back_copy(p, me).wait_send())
+    peers(lambda p: side_copy(p, me).wait_send())
+    for h in pieces:
+        peers(lambda p: trace_copy(h, p, me).wait_send())
+        peers(lambda p: proj_copy(h, p, me).wait_send())
+        peers(lambda p: back_copy(h, p, me).wait_send())
     for q in partners:
         tm_copy(0, pow_out, pow_in, q, core).wait_send()
         tm_copy(1, num_out, num_in, q, core).wait_send()
@@ -268,6 +298,7 @@
     slots = footprints.shape[0]
     neur, frames = traces.shape
     padded = n * ROWS
+    wide = frames // PARTS
     return pl.pallas_call(
         functools.partial(kernel, n, t),
         out_shape=(
@@ -282,23 +313,27 @@
             pltpu.VMEM((1, slots), jnp.int32),
             pltpu.VMEM((1, slots), jnp.int32),
             pltpu.VMEM((1, n), jnp.int32),
-            pltpu.VMEM((n * neur, frames), BF16),
-            pltpu.VMEM((padded, frames + SIDE), BF16),
-            pltpu.VMEM((padded, frames + SIDE), BF16),
-            pltpu.VMEM((padded, frames), BF16),
-            pltpu.VMEM((padded, frames), BF16),
+            pltpu.VMEM((PARTS, n * neur, wide), BF16),
+            pltpu.VMEM((n, 1, LANES), F32),
+            pltpu.VMEM((n, 1, LANES), F32),
+            pltpu.VMEM((PARTS, padded, wide), BF16),
+            pltpu.VMEM((PARTS, padded, wide), BF16),
+            pltpu.VMEM((PARTS, padded, wide), BF16),
+            pltpu.VMEM((PARTS, padded, wide), BF16),
             pltpu.VMEM((slots, BLOCK), F32),
             pltpu.VMEM((t, slots, BLOCK), F32),
             pltpu.VMEM((slots, BLOCK), F32),
             pltpu.VMEM((t, slots, BLOCK), F32),
-            pltpu.SemaphoreType.DMA((6,)),
-            pltpu.SemaphoreType.DMA((3, n)),
-            pltpu.SemaphoreType.DMA((3, n)),
+            pltpu.SemaphoreType.DMA((5 + PARTS,)),
+            pltpu.SemaphoreType.DMA((3, PARTS, n)),
+            pltpu.SemaphoreType.DMA((3, PARTS, n)),
+            pltpu.SemaphoreType.DMA((n,)),
+            pltpu.SemaphoreType.DMA((n,)),
             pltpu.SemaphoreType.DMA((2, t)),
             pltpu.SemaphoreType.DMA((2, t)),
         ],
         compiler_params=pltpu.CompilerParams(
-            collective_id=0, has_side_effects=True, vmem_limit_bytes=48 * 1024 * 1024
+            collective_id=0, has_side_effects=True, vmem_limit_bytes=64 * 1024 * 1024 - 256 * 1024
         ),
     )(
         movie,

time: 34.1 us -> 32.4 us (0.950)
  local copies, waits for them, and re-layouts: 4.72 us -> 2.89 us
    unnamed x14 -> x2, local copies, waits for them, and re-layouts: 4.72 us -> 2.89 us
where the time goes in v2:
time: 32.4 us; the launch traced here: 32.1 us
  Pallas kernels  28.5 us (88%)
  local copies, waits for them, and re-layouts  2.89 us (9%)
  between operations  0.64 us (2%)
    pallas_call x1, Pallas kernels, local(): pl.pallas_call(functools.partial(kernel, n, t), out_shape=(jax.ShapeDtype...  28.5 us
    unnamed x2, local copies, waits for them, and re-layouts  2.89 us

profile of v2, /device:TPU:0, one launch (start us, length us, event | category | flops | bytes accessed | tf_op | source)
XLA Modules:
  0.0 32.1 jit_solution(16014884218062503876)
XLA Ops:
  0.6 28.5 %shard_map.77 = (bf16[32,256]{1,0:T(8,128)(2,1)}, f32[256,128]{1,0:T(8,128)}) custom-call(bf16[2048,256]{1,0:T(8,128)(2,1)} %movie_hbm.1, bf16[32,256]{1,0:T(8,128)(2,1)} %traces_hbm.1, bf16[256,128]{1,0:T(8,128)(2,1)} %foot_hbm.1, s32[1,256]{1,0:T(1,128)} %bitcast.2, s32[1,256]{1,0:T(1,128)} %bitcast.3, s32[1,16]{1,0:T(1,128)} %fill_hbm.1), custom_call_target="tpu_custom_call" | custom-call | tf_op jit(solution)/shard_map/pallas_call | solution.py:302
  29.2 1.3 %copy.10 = bf16[32,256]{1,0:T(8,128)(2,1)} copy(bf16[32,256]{1,0:T(8,128)(2,1)} %get-tuple-element.4) | data formatting | bytes 32768
  30.5 1.6 %copy.11 = f32[256,128]{1,0:T(8,128)} copy(f32[256,128]{1,0:T(8,128)} %get-tuple-element.5) | data formatting | bytes 262144

commit v3 on v2

--- a/solution.py
+++ b/solution.py
@@ -10,7 +10,7 @@
 BLOCK = 128
 ROWS = 16
 LANES = 128
-PARTS = 1
+PARTS = 2
 F32 = jnp.float32
 BF16 = jnp.bfloat16
 NN = (((1,), (0,)), ((), ()))

time: 32.4 us -> 32.4 us (level)
  no operation moved by 1% of the time
where the time goes in v3:
time: 32.4 us; the launch traced here: 32.1 us
  Pallas kernels  28.5 us (88%)
  local copies, waits for them, and re-layouts  2.89 us (9%)
  between operations  0.64 us (2%)
    pallas_call x1, Pallas kernels, local(): pl.pallas_call(functools.partial(kernel, n, t), out_shape=(jax.ShapeDtype...  28.5 us
    unnamed x2, local copies, waits for them, and re-layouts  2.89 us

profile of v3, /device:TPU:0, one launch (start us, length us, event | category | flops | bytes accessed | tf_op | source)
XLA Modules:
  0.0 32.1 jit_solution(8646588054966245709)
XLA Ops:
  0.6 28.5 %shard_map.77 = (bf16[32,256]{1,0:T(8,128)(2,1)}, f32[256,128]{1,0:T(8,128)}) custom-call(bf16[2048,256]{1,0:T(8,128)(2,1)} %movie_hbm.1, bf16[32,256]{1,0:T(8,128)(2,1)} %traces_hbm.1, bf16[256,128]{1,0:T(8,128)(2,1)} %foot_hbm.1, s32[1,256]{1,0:T(1,128)} %bitcast.2, s32[1,256]{1,0:T(1,128)} %bitcast.3, s32[1,16]{1,0:T(1,128)} %fill_hbm.1), custom_call_target="tpu_custom_call" | custom-call | tf_op jit(solution)/shard_map/pallas_call | solution.py:302
  29.2 1.3 %copy.10 = bf16[32,256]{1,0:T(8,128)(2,1)} copy(bf16[32,256]{1,0:T(8,128)(2,1)} %get-tuple-element.4) | data formatting | bytes 32768
  30.5 1.6 %copy.11 = f32[256,128]{1,0:T(8,128)} copy(f32[256,128]{1,0:T(8,128)} %get-tuple-element.5) | data formatting | bytes 262144

commit v4 on v2

--- a/solution.py
+++ b/solution.py
@@ -11,6 +11,7 @@
 ROWS = 16
 LANES = 128
 PARTS = 1
+VMEM_BYTES = 64 * 1024 * 1024 - 256 * 1024
 F32 = jnp.float32
 BF16 = jnp.bfloat16
 NN = (((1,), (0,)), ((), ()))
@@ -60,6 +61,10 @@
     wide = frames // PARTS
     pieces = range(PARTS)
 
+    def wait_rest(ref, sem, rows):
+        rest = ref.at[pl.ds(0, (n - 1) * rows)]
+        pltpu.make_async_copy(rest, rest, sem).wait()
+
     def pix_id(peer):
         return (peer, core)
 
@@ -107,8 +112,8 @@
         return pltpu.make_async_remote_copy(
             src_ref=mine(h),
             dst_ref=all_traces.at[h, part(source, neur)],
-            send_sem=send_sem.at[0, h, p],
-            recv_sem=recv_sem.at[0, h, source],
+            send_sem=send_sem.at[0, h],
+            recv_sem=recv_sem.at[0, h],
             device_id=pix_id(p),
         )
 
@@ -147,8 +152,8 @@
         return pltpu.make_async_remote_copy(
             src_ref=side_out.at[p],
             dst_ref=side_in.at[source],
-            send_sem=side_send.at[p],
-            recv_sem=side_recv.at[source],
+            send_sem=side_send.at[0],
+            recv_sem=side_recv.at[0],
             device_id=pix_id(p),
         )
 
@@ -190,20 +195,20 @@
         return pltpu.make_async_remote_copy(
             src_ref=proj_out.at[h, part(p, ROWS)],
             dst_ref=proj_in.at[h, part(source, ROWS)],
-            send_sem=send_sem.at[1, h, p],
-            recv_sem=recv_sem.at[1, h, source],
+            send_sem=send_sem.at[1, h],
+            recv_sem=recv_sem.at[1, h],
             device_id=pix_id(p),
         )
 
     for h in pieces:
-        peers(lambda p: trace_copy(h, p, p).wait_recv())
+        wait_rest(all_traces.at[h], recv_sem.at[0, h], neur)
         gathered = all_traces[h]
         projection = base[:, strip(h)] - (dot(couple_high, gathered) + dot(couple_low, gathered))
         proj_out[h] = widen(projection.astype(BF16))
         peers(lambda p: proj_copy(h, p, me).start())
         proj_in[h, part(me, ROWS), :] = proj_out[h, part(me, ROWS), :]
 
-    peers(lambda p: side_copy(p, p).wait_recv())
+    wait_rest(side_in, side_recv.at[0], 1)
     side_rows = jnp.concatenate([side_in[i] for i in range(n)], axis=0)
     from_tile = (lax.div(iota((padded, n), 0), ROWS) == iota((padded, n), 1)).astype(BF16)
     spread = exact_dot(from_tile, side_rows)
@@ -225,13 +230,13 @@
         return pltpu.make_async_remote_copy(
             src_ref=back_out.at[h, part(p, ROWS)],
             dst_ref=back_in.at[h, part(source, ROWS)],
-            send_sem=send_sem.at[2, h, p],
-            recv_sem=recv_sem.at[2, h, source],
+            send_sem=send_sem.at[2, h],
+            recv_sem=recv_sem.at[2, h],
             device_id=pix_id(p),
         )
 
     for h in pieces:
-        peers(lambda p: proj_copy(h, p, p).wait_recv())
+        wait_rest(proj_in.at[h], recv_sem.at[1, h], ROWS)
         own = all_traces[h, part(me, neur), :].astype(F32)
         sums = dot(pick_turned, proj_in[h])
         updated = jnp.maximum(0.0, own + sums / floor_power).astype(BF16)
@@ -241,7 +246,7 @@
         new_ref[:, strip(h)] = updated
 
     for h in pieces:
-        peers(lambda p: back_copy(h, p, p).wait_recv())
+        wait_rest(back_in.at[h], recv_sem.at[2, h], ROWS)
     fresh = jnp.concatenate([narrow(back_in[h]) for h in pieces], axis=1)
     fresh_f = fresh.astype(F32)
     pow_out[...] = jnp.broadcast_to(
@@ -284,14 +289,25 @@
     grown = jnp.maximum(0.0, masked + num_all / (pow_all + 1e-06))
     grown_ref[...] = jnp.where(usable, grown, 0.0)
 
-    peers(lambda p: side_copy(p, me).wait_send())
-    for h in pieces:
-        peers(lambda p: trace_copy(h, p, me).wait_send())
-        peers(lambda p: proj_copy(h, p, me).wait_send())
-        peers(lambda p: back_copy(h, p, me).wait_send())
+    wait_rest(side_out, side_send.at[0], 1)
+    for h in pieces:
+        wait_rest(all_traces.at[h], send_sem.at[0, h], neur)
+        wait_rest(proj_out.at[h], send_sem.at[1, h], ROWS)
+        wait_rest(back_out.at[h], send_sem.at[2, h], ROWS)
     for q in partners:
         tm_copy(0, pow_out, pow_in, q, core).wait_send()
         tm_copy(1, num_out, num_in, q, core).wait_send()
+
+
+def settle(new_in, grown_in, new_out, grown_out, sem):
+    moves = [
+        pltpu.make_async_copy(new_in, new_out, sem.at[0]),
+        pltpu.make_async_copy(grown_in, grown_out, sem.at[1]),
+    ]
+    for move in moves:
+        move.start()
+    for move in moves:
+        move.wait()
 
 
 def local(n, t, movie, traces, footprints, slot_block, slot_neuron, bucket_fill):
@@ -299,12 +315,13 @@
     neur, frames = traces.shape
     padded = n * ROWS
     wide = frames // PARTS
-    return pl.pallas_call(
+    results = (
+        jax.ShapeDtypeStruct((neur, frames), BF16),
+        jax.ShapeDtypeStruct((slots, BLOCK), F32),
+    )
+    swept = pl.pallas_call(
         functools.partial(kernel, n, t),
-        out_shape=(
-            jax.ShapeDtypeStruct((neur, frames), BF16),
-            jax.ShapeDtypeStruct((slots, BLOCK), F32),
-        ),
+        out_shape=results,
         in_specs=[pl.BlockSpec(memory_space=pl.ANY)] * 6,
         out_specs=[pl.BlockSpec(memory_space=pltpu.VMEM)] * 2,
         scratch_shapes=[
@@ -325,15 +342,15 @@
             pltpu.VMEM((slots, BLOCK), F32),
             pltpu.VMEM((t, slots, BLOCK), F32),
             pltpu.SemaphoreType.DMA((5 + PARTS,)),
-            pltpu.SemaphoreType.DMA((3, PARTS, n)),
-            pltpu.SemaphoreType.DMA((3, PARTS, n)),
-            pltpu.SemaphoreType.DMA((n,)),
-            pltpu.SemaphoreType.DMA((n,)),
+            pltpu.SemaphoreType.DMA((3, PARTS)),
+            pltpu.SemaphoreType.DMA((3, PARTS)),
+            pltpu.SemaphoreType.DMA((1,)),
+            pltpu.SemaphoreType.DMA((1,)),
             pltpu.SemaphoreType.DMA((2, t)),
             pltpu.SemaphoreType.DMA((2, t)),
         ],
         compiler_params=pltpu.CompilerParams(
-            collective_id=0, has_side_effects=True, vmem_limit_bytes=64 * 1024 * 1024 - 256 * 1024
+            collective_id=0, has_side_effects=True, vmem_limit_bytes=VMEM_BYTES
         ),
     )(
         movie,
@@ -343,6 +360,14 @@
         slot_neuron.reshape(1, slots),
         bucket_fill,
     )
+    return pl.pallas_call(
+        settle,
+        out_shape=results,
+        in_specs=[pl.BlockSpec(memory_space=pl.ANY)] * 2,
+        out_specs=[pl.BlockSpec(memory_space=pl.ANY)] * 2,
+        scratch_shapes=[pltpu.SemaphoreType.DMA((2,))],
+        compiler_params=pltpu.CompilerParams(vmem_limit_bytes=VMEM_BYTES),
+    )(*swept)
 
 
 def solution(mesh):

time: 32.4 us -> 33.9 us (1.046)
  Pallas kernels: 28.5 us -> 33 us
  local copies, waits for them, and re-layouts: 2.89 us -> 0 us
    pallas_call x1 -> x2, Pallas kernels: 28.5 us -> 33 us  [the longest x1 27.4 us: local(): pl.pallas_call(functools.partial(kernel, n, t), out_shape=results, in_spe...]
    unnamed x2 -> x0, local copies, waits for them, and re-layouts: 2.89 us -> none
where the time goes in v4:
time: 33.9 us; the launch traced here: 33.7 us
  Pallas kernels  33 us (97%)
  between operations  0.64 us (2%)
    pallas_call x1, Pallas kernels, local(): pl.pallas_call(functools.partial(kernel, n, t), out_shape=results, in_spe...  27.4 us
    pallas_call x1, Pallas kernels, local(): pl.pallas_call(settle, out_shape=results, in_specs=[pl.BlockSpec(memory_s...  5.59 us

profile of v4, /device:TPU:0, one launch (start us, length us, event | category | flops | bytes accessed | tf_op | source)
XLA Modules:
  0.0 33.7 jit_solution(5383707311808477917)
XLA Ops:
  0.6 27.4 %shard_map.77 = (bf16[32,256]{1,0:T(8,128)(2,1)}, f32[256,128]{1,0:T(8,128)}) custom-call(bf16[2048,256]{1,0:T(8,128)(2,1)} %movie_hbm.1, bf16[32,256]{1,0:T(8,128)(2,1)} %traces_hbm.1, bf16[256,128]{1,0:T(8,128)(2,1)} %foot_hbm.1, s32[1,256]{1,0:T(1,128)} %bitcast.2, s32[1,256]{1,0:T(1,128)} %bitcast.3, s32[1,16]{1,0:T(1,128)} %fill_hbm.1), custom_call_target="tpu_custom_call" | custom-call | tf_op jit(solution)/shard_map/pallas_call | solution.py:322
  28.1 5.6 %shard_map.78 = (bf16[32,256]{1,0:T(8,128)(2,1)}, f32[256,128]{1,0:T(8,128)}) custom-call(bf16[32,256]{1,0:T(8,128)(2,1)} %get-tuple-element.4.new_in, f32[256,128]{1,0:T(8,128)} %get-tuple-element.5.grown_in), custom_call_target="tpu_custom_call" | custom-call | tf_op jit(solution)/shard_map/pallas_call | solution.py:363

commit v5 on v4

--- a/solution.py
+++ b/solution.py
@@ -10,7 +10,7 @@
 BLOCK = 128
 ROWS = 16
 LANES = 128
-PARTS = 1
+PARTS = 2
 VMEM_BYTES = 64 * 1024 * 1024 - 256 * 1024
 F32 = jnp.float32
 BF16 = jnp.bfloat16
@@ -299,15 +299,9 @@
         tm_copy(1, num_out, num_in, q, core).wait_send()
 
 
-def settle(new_in, grown_in, new_out, grown_out, sem):
-    moves = [
-        pltpu.make_async_copy(new_in, new_out, sem.at[0]),
-        pltpu.make_async_copy(grown_in, grown_out, sem.at[1]),
-    ]
-    for move in moves:
-        move.start()
-    for move in moves:
-        move.wait()
+def settle(new_in, grown_in, new_out, grown_out):
+    new_out[...] = new_in[...]
+    grown_out[...] = grown_in[...]
 
 
 def local(n, t, movie, traces, footprints, slot_block, slot_neuron, bucket_fill):
@@ -363,9 +357,8 @@
     return pl.pallas_call(
         settle,
         out_shape=results,
-        in_specs=[pl.BlockSpec(memory_space=pl.ANY)] * 2,
-        out_specs=[pl.BlockSpec(memory_space=pl.ANY)] * 2,
-        scratch_shapes=[pltpu.SemaphoreType.DMA((2,))],
+        in_specs=[pl.BlockSpec(memory_space=pltpu.VMEM)] * 2,
+        out_specs=[pl.BlockSpec(memory_space=pltpu.VMEM)] * 2,
         compiler_params=pltpu.CompilerParams(vmem_limit_bytes=VMEM_BYTES),
     )(*swept)
 

time: 33.9 us -> 29.1 us (0.86)
  Pallas kernels: 33 us -> 28.2 us
    pallas_call x1, Pallas kernels: 5.59 us -> 1.59 us  [local(): pl.pallas_call(settle, out_shape=results, in_specs=[pl.BlockSpec(memory_s...]
    pallas_call x1, Pallas kernels: 27.4 us -> 26.6 us  [local(): pl.pallas_call(functools.partial(kernel, n, t), out_shape=results, in_spe...]
where the time goes in v5:
time: 29.1 us; the launch traced here: 28.9 us
  Pallas kernels  28.2 us (97%)
  between operations  0.64 us (2%)
    pallas_call x1, Pallas kernels, local(): pl.pallas_call(functools.partial(kernel, n, t), out_shape=results, in_spe...  26.6 us
    pallas_call x1, Pallas kernels, local(): pl.pallas_call(settle, out_shape=results, in_specs=[pl.BlockSpec(memory_s...  1.59 us

profile of v5, /device:TPU:0, one launch (start us, length us, event | category | flops | bytes accessed | tf_op | source)
XLA Modules:
  0.0 28.9 jit_solution(7721558487853820318)
XLA Ops:
  0.6 26.6 %shard_map.77 = (bf16[32,256]{1,0:T(8,128)(2,1)}, f32[256,128]{1,0:T(8,128)}) custom-call(bf16[2048,256]{1,0:T(8,128)(2,1)} %movie_hbm.1, bf16[32,256]{1,0:T(8,128)(2,1)} %traces_hbm.1, bf16[256,128]{1,0:T(8,128)(2,1)} %foot_hbm.1, s32[1,256]{1,0:T(1,128)} %bitcast.2, s32[1,256]{1,0:T(1,128)} %bitcast.3, s32[1,16]{1,0:T(1,128)} %fill_hbm.1), custom_call_target="tpu_custom_call" | custom-call | tf_op jit(solution)/shard_map/pallas_call | solution.py:316
  27.3 1.6 %shard_map.78 = (bf16[32,256]{1,0:T(8,128)(2,1)}, f32[256,128]{1,0:T(8,128)}) custom-call(bf16[32,256]{1,0:T(8,128)(2,1)} %get-tuple-element.4.new_in, f32[256,128]{1,0:T(8,128)} %get-tuple-element.5.grown_in), custom_call_target="tpu_custom_call" | custom-call | tf_op jit(solution)/shard_map/pallas_call | solution.py:357

commit v6 on v5

--- a/solution.py
+++ b/solution.py
@@ -11,6 +11,7 @@
 ROWS = 16
 LANES = 128
 PARTS = 2
+PLANE = 4
 VMEM_BYTES = 64 * 1024 * 1024 - 256 * 1024
 F32 = jnp.float32
 BF16 = jnp.bfloat16
@@ -48,7 +49,7 @@
     movie, foot, block_ref, neuron_ref, fill_ref,
     all_traces, side_out, side_in, proj_out, proj_in, back_out, back_in,
     num_out, num_in, pow_out, pow_in,
-    local_sem, send_sem, recv_sem, side_send, side_recv, tm_send, tm_recv,
+    local_sem, send_sem, recv_sem, column_sem, side_send, side_recv, tm_send, tm_recv,
 ):
     me = lax.axis_index("pix")
     core = lax.axis_index("tm")
@@ -61,8 +62,8 @@
     wide = frames // PARTS
     pieces = range(PARTS)
 
-    def wait_rest(ref, sem, rows):
-        rest = ref.at[pl.ds(0, (n - 1) * rows)]
+    def wait_rest(ref, sem, rows, count=n - 1):
+        rest = ref.at[pl.ds(0, count * rows)]
         pltpu.make_async_copy(rest, rest, sem).wait()
 
     def pix_id(peer):
@@ -108,17 +109,30 @@
         loads[h].wait()
     pl.semaphore_wait(barrier, n - 1 + t - 1)
 
-    def trace_copy(h, p, source):
+    planes = n // PLANE
+    plane, spot = lax.div(me, PLANE), lax.rem(me, PLANE)
+
+    def trace_copy(h, source, p, sem):
         return pltpu.make_async_remote_copy(
-            src_ref=mine(h),
+            src_ref=all_traces.at[h, part(source, neur)],
             dst_ref=all_traces.at[h, part(source, neur)],
             send_sem=send_sem.at[0, h],
-            recv_sem=recv_sem.at[0, h],
+            recv_sem=sem,
             device_id=pix_id(p),
         )
 
-    for h in pieces:
-        peers(lambda p: trace_copy(h, p, me).start())
+    def spread_plane(h, source):
+        for k in range(1, PLANE):
+            p = plane * PLANE + lax.rem(spot + k, PLANE)
+            trace_copy(h, source, p, recv_sem.at[0, h]).start()
+
+    def column_peer(k):
+        return lax.rem(plane + k, planes) * PLANE + spot
+
+    for h in pieces:
+        for k in near_order(planes):
+            trace_copy(h, me, column_peer(k), column_sem.at[h, k]).start()
+        spread_plane(h, me)
     for load in loads[PARTS:-1]:
         load.wait()
 
@@ -176,6 +190,12 @@
         def narrow(x):
             return dot(place, x, TN).astype(BF16)
 
+    for h in pieces:
+        for k in near_order(planes):
+            source = column_peer(planes - k)
+            trace_copy(h, source, source, column_sem.at[h, k]).wait_recv()
+            spread_plane(h, source)
+
     gram = jnp.where(same_block, dot(masked_b, masked_b, NT), 0.0)
     neuron_id = lax.div(row_of, cap).astype(F32) * neur + neuron_col
     pick = (neuron_id == iota((slots, neurons), 1).astype(F32)).astype(BF16)
@@ -201,7 +221,7 @@
         )
 
     for h in pieces:
-        wait_rest(all_traces.at[h], recv_sem.at[0, h], neur)
+        wait_rest(all_traces.at[h], recv_sem.at[0, h], neur, n - planes)
         gathered = all_traces[h]
         projection = base[:, strip(h)] - (dot(couple_high, gathered) + dot(couple_low, gathered))
         proj_out[h] = widen(projection.astype(BF16))
@@ -338,6 +358,7 @@
             pltpu.SemaphoreType.DMA((5 + PARTS,)),
             pltpu.SemaphoreType.DMA((3, PARTS)),
             pltpu.SemaphoreType.DMA((3, PARTS)),
+            pltpu.SemaphoreType.DMA((PARTS, n // PLANE)),
             pltpu.SemaphoreType.DMA((1,)),
             pltpu.SemaphoreType.DMA((1,)),
             pltpu.SemaphoreType.DMA((2, t)),

time: 29.1 us -> 28.6 us (0.983)
  Pallas kernels: 28.2 us -> 27.7 us
    pallas_call x1, Pallas kernels: 26.6 us -> 26.2 us  [local(): pl.pallas_call(functools.partial(kernel, n, t), out_shape=results, in_spe...]
where the time goes in v6:
time: 28.6 us; the launch traced here: 28.4 us
  Pallas kernels  27.7 us (97%)
  between operations  0.64 us (2%)
    pallas_call x1, Pallas kernels, local(): pl.pallas_call(functools.partial(kernel, n, t), out_shape=results, in_spe...  26.2 us
    pallas_call x1, Pallas kernels, local(): pl.pallas_call(settle, out_shape=results, in_specs=[pl.BlockSpec(memory_s...  1.59 us

profile of v6, /device:TPU:0, one launch (start us, length us, event | category | flops | bytes accessed | tf_op | source)
XLA Modules:
  0.0 28.4 jit_solution(15283284565652763125)
XLA Ops:
  0.6 26.2 %shard_map.77 = (bf16[32,256]{1,0:T(8,128)(2,1)}, f32[256,128]{1,0:T(8,128)}) custom-call(bf16[2048,256]{1,0:T(8,128)(2,1)} %movie_hbm.1, bf16[32,256]{1,0:T(8,128)(2,1)} %traces_hbm.1, bf16[256,128]{1,0:T(8,128)(2,1)} %foot_hbm.1, s32[1,256]{1,0:T(1,128)} %bitcast.2, s32[1,256]{1,0:T(1,128)} %bitcast.3, s32[1,16]{1,0:T(1,128)} %fill_hbm.1), custom_call_target="tpu_custom_call" | custom-call | tf_op jit(solution)/shard_map/pallas_call | solution.py:336
  26.8 1.6 %shard_map.78 = (bf16[32,256]{1,0:T(8,128)(2,1)}, f32[256,128]{1,0:T(8,128)}) custom-call(bf16[32,256]{1,0:T(8,128)(2,1)} %get-tuple-element.4.new_in, f32[256,128]{1,0:T(8,128)} %get-tuple-element.5.grown_in), custom_call_target="tpu_custom_call" | custom-call | tf_op jit(solution)/shard_map/pallas_call | solution.py:378
